TPU v7x, 32 devices: a whole 2x2x4 slice. The times are simulated.
32 devices in a mesh: grp: 2 (over y), seg: 2 (over core), inner: 8 (over z, x).
Axes of the slice: x: 2, y: 2, z: 4, core: 2. Of those that a mesh axis runs over, the one named last changes fastest.
Arguments:
- queries: bfloat16 [8192, 8, 128], P(('grp', 'seg', 'inner')), parts along dimension 0, may hold values from -5.5 to 5.5
- keys: bfloat16 [8192, 8, 128], P(('grp', 'seg', 'inner')), parts along dimension 0, may hold values from -6 to 6
- values: bfloat16 [8192, 8, 128], P(('grp', 'seg', 'inner')), parts along dimension 0, may hold values from -6 to 6
- strengths: float32 [8192, 8], P(('grp', 'seg', 'inner')), parts along dimension 0, may hold values from 0.001 to 1.95, as said below
Outputs:
- outputs: bfloat16 [8192, 8, 128], P(('grp', 'seg', 'inner')), parts along dimension 0
There are 2 independent parts, one for each index of `grp`. A program takes and returns all parts, laid end to end along the dimension named above; each array names one. Nothing has to cross between parts.
Inputs may be any that keep to these rules, and one draw needn't show every extreme that they name: Positive reflection strengths; a head's strengths lie within a factor of three of each other.
All inputs are finite; a program needn't handle non-finite values.
Results may differ from a plain program's by a relative error of at most 0.001.
Values sent between devices are 32-bit elements; how exact they have to be, the bound alone decides.
A program may use at most 512 MiB of HBM per device.

v0:
```python
import jax
import jax.numpy as jnp
from jax import lax
from jax.sharding import PartitionSpec as P


def entering(part, axis, combine, identity):
    place = lax.axis_index(axis)
    gathered = jax.tree.map(lambda a: lax.all_gather(a, axis), part)
    state = jax.tree.map(lambda a, e: jnp.zeros_like(a) + jnp.asarray(e, a.dtype), part, identity)

    def one(hop, state):
        return combine(
            state, jax.tree.map(lambda a: lax.dynamic_index_in_dim(a, hop, 0, False), gathered)
        )

    return lax.fori_loop(0, place, one, state)


def unit_rows(field):
    field = field.astype(jnp.float32)
    return field * lax.rsqrt(jnp.sum(field * field, axis=-1, keepdims=True) + 1e-06)


def block_terms(queries, keys, values, strengths):
    hp = lax.Precision.HIGHEST
    query_h = jnp.transpose(unit_rows(queries), (1, 0, 2))
    key_h = jnp.transpose(unit_rows(keys), (1, 0, 2))
    value_h = jnp.transpose(values.astype(jnp.float32), (1, 0, 2))
    beta_h = jnp.transpose(strengths, (1, 0))[:, :, None]
    rows = key_h.shape[1]
    gram = jnp.einsum("hid,hjd->hij", key_h, key_h, precision=hp)
    lower = jnp.tril(gram, -1) * beta_h
    system = jnp.eye(rows, dtype=jnp.float32)[None] + lower
    right = jnp.concatenate([beta_h * value_h, beta_h * key_h], axis=-1)
    solved = jax.scipy.linalg.solve_triangular(system, right, lower=True, unit_diagonal=True)
    width_v = value_h.shape[2]
    ubar = solved[..., :width_v]
    wmat = solved[..., width_v:]
    scores = jnp.tril(jnp.einsum("hid,hjd->hij", query_h, key_h, precision=hp))
    local_out = jnp.einsum("hij,hjv->hiv", scores, ubar, precision=hp)
    query_fix = query_h - jnp.einsum("hij,hjd->hid", scores, wmat, precision=hp)
    width_k = key_h.shape[2]
    trans = jnp.eye(width_k, dtype=jnp.float32)[None] - jnp.einsum(
        "hcd,hce->hde", wmat, key_h, precision=hp
    )
    offset = jnp.einsum("hcv,hcd->hvd", ubar, key_h, precision=hp)
    return (trans, offset, local_out, query_fix)


def compose(earlier, later):
    hp = lax.Precision.HIGHEST
    trans = jnp.einsum("hde,hef->hdf", earlier[0], later[0], precision=hp)
    offset = jnp.einsum("hve,hef->hvf", earlier[1], later[0], precision=hp) + later[1]
    return (trans, offset)


def apply_map(state, trans, offset):
    return jnp.einsum("hvd,hde->hve", state, trans, precision=lax.Precision.HIGHEST) + offset


def body(queries, keys, values, strengths):
    hp = lax.Precision.HIGHEST
    rows = queries.shape[0]
    head_count = queries.shape[1]
    width_k = queries.shape[2]
    width_v = values.shape[2]
    block = min(128, rows)
    count = rows // block
    qs = queries.reshape(count, block, head_count, width_k)
    ks = keys.reshape(count, block, head_count, width_k)
    vs = values.reshape(count, block, head_count, width_v)
    bs = strengths.reshape(count, block, head_count)

    def terms_of(pieces):
        return block_terms(pieces[0], pieces[1], pieces[2], pieces[3])

    all_trans, all_offset, all_local, all_fix = lax.map(terms_of, (qs, ks, vs, bs))
    identity = (
        jnp.broadcast_to(jnp.eye(width_k, dtype=jnp.float32), (head_count, width_k, width_k)),
        jnp.zeros((head_count, width_v, width_k), jnp.float32),
    )

    def fold_maps(carry, pieces):
        return (compose(carry, pieces), None)

    shard_map_total, unused = lax.scan(fold_maps, identity, (all_trans, all_offset))
    trans, offset = shard_map_total
    before_trans, before_offset = entering((trans, offset), ("seg", "inner"), compose, identity)

    def emit(carry, pieces):
        result = pieces[2] + jnp.einsum("hcd,hvd->hcv", pieces[3], carry, precision=hp)
        carry = apply_map(carry, pieces[0], pieces[1])
        return (carry, jnp.transpose(result, (1, 0, 2)).astype(jnp.bfloat16))

    final, blocks = lax.scan(emit, before_offset, (all_trans, all_offset, all_local, all_fix))
    return blocks.reshape(rows, head_count, width_v)


def solution(mesh):
    placed = (
        P(("grp", "seg", "inner"), None, None),
        P(("grp", "seg", "inner"), None, None),
        P(("grp", "seg", "inner"), None, None),
        P(("grp", "seg", "inner"), None),
    )
    return jax.shard_map(
        body,
        mesh=mesh,
        in_specs=placed,
        out_specs=P(("grp", "seg", "inner"), None, None),
        check_vma=False,
    )
```

profile of v0, /device:TPU:25, one launch (start us, length us, event | category | flops | bytes accessed | tf_op | source)
XLA Modules:
  0.0 423.2 jit_solution(14396319787075859885)
XLA Ops:
  6.6 193.7 %while.53 = (s32[]{:T(128)}, f32[2,8,128,128]{2,3,1,0:T(8,128)S(1)}, f32[2,8,128,128]{2,3,1,0:T(8,128)}, f32[2,8,128,128]{3,2,1,0:T(8,128)}, f32[2,8,128,128]{3,...) while((s32[]{:T(128)}, ...), condition=%wide.region_3.4_spmd, body=%wide.region_0.3_spmd.sunk | while | flops 1615036544 | bytes 16718453 | solution.py:78
  12.2 79.2 %custom-call.11 = f32[8,1,128,128]{2,3,1,0:T(8,128)} custom-call(f32[8,1,128,128]{3,2,1,0:T(8,128)S(1)} %fusion.122), custom_call_target="InvertDiagBlocksLowerTriangular" | custom-call | tf_op jit(solution)/shard_map/while/body/eval_jaxpr/jit(_solve_triangular)/vmap()/triangular_solve | solution.py:36
  91.4 2.2 fusion.123
  101.4 2.0 fusion.125
  109.0 79.2 %custom-call.11 = f32[8,1,128,128]{2,3,1,0:T(8,128)} custom-call(f32[8,1,128,128]{3,2,1,0:T(8,128)S(1)} %fusion.122), custom_call_target="InvertDiagBlocksLowerTriangular" | custom-call | tf_op jit(solution)/shard_map/while/body/eval_jaxpr/jit(_solve_triangular)/vmap()/triangular_solve | solution.py:36
  188.3 2.2 fusion.123
  198.3 2.0 fusion.125
  200.3 8.5 %while.56 = (s32[]{:T(128)}, f32[8,128,128]{1,2,0:T(8,128)S(1)}, f32[8,128,128]{1,2,0:T(8,128)}, f32[2,8,128,128]{2,3,1,0:T(8,128)S(1)}, f32[2,8,128,128]{2,3,1,0:T(8,128)}, /*index=5*/s32[]{:T(128)}, s32[]{:T(128)}) while((s32[]{:T(128)}, f32[8,128,128]{1,2,0:T(8,128)S(1)}, f32[8,128,128]{1,2,0:T(8,128)}, ...), condition=%wide.region_5.6_spmd.clone, body=%wide.region_4.5_spmd.clone.sunk | while | flops 402915328 | bytes 5768283 | solution.py:87
  201.3 2.5 fusion.142
  205.6 2.5 fusion.142
  210.0 2.0 copy.48
  212.1 72.3 %all-gather.5.cloned.1.call-done = f32[128,128,128]{2,1,0:T(8,128)} async-done(((f32[8,128,128]{2,1,0:T(8,128)}), f32[128,128,128]{2,1,0:T(8,128)}) %all-gather.5.cloned.1.call-update) | async-done | bytes 8388624 | tf_op jit(solution)/shard_map/all_gather | solution.py:9
  284.5 75.4 %all-gather.7.cloned.1.call-done = f32[128,128,128]{2,1,0:T(8,128)} async-done(((f32[8,128,128]{2,1,0:T(8,128)}), f32[128,128,128]{2,1,0:T(8,128)}) %all-gather.7.cloned.1.call-update) | async-done | bytes 8388624 | tf_op jit(solution)/shard_map/all_gather | solution.py:9
  359.9 48.0 %while.54 = (s32[]{:T(128)}, f32[8,128,128]{1,2,0:T(8,128)S(1)}, s32[]{:T(128)}, f32[16,8,128,128]{3,2,1,0:T(8,128)}, f32[16,8,128,128]{3,2,1,0:T(8,128)}, /*index=5*/s32[]{:T(128)}, s32[]{:T(128)}, s32[]{:T(128)}) while((s32[]{:T(128)}, f32[8,128,128]{1,2,0:T(8,128)S(1)}, s32[]{:T(128)}, f32[16,8,128,128]{3,2,1,0:T(8,128)}, ...), condition=%wide.region_7.8_spmd, body=%wide.region_6.7_spmd.sunk | while | flops 201457664 | bytes 5243007 | solution.py:17
  361.2 2.1 fusion.131
  364.7 2.1 fusion.131
  368.1 2.1 fusion.131
  371.5 2.1 fusion.131
  375.0 2.1 fusion.131
  378.4 2.1 fusion.131
  381.8 2.1 fusion.131
  385.2 2.1 fusion.131
  388.7 2.1 fusion.131
  392.1 2.1 fusion.131
  395.5 2.1 fusion.131
  399.0 2.1 fusion.131
  402.4 2.1 fusion.131
  405.8 2.1 fusion.131
  407.9 7.6 %while.55 = (s32[]{:T(128)}, f32[8,128,128]{1,2,0:T(8,128)S(1)}, bf16[2,128,8,128]{3,2,1,0:T(8,128)(2,1)S(1)}, f32[2,8,128,128]{2,3,1,0:T(8,128)S(1)}, f32[2,8,1...) while((s32[]{:T(128)}, f32[8,128,128]{1,2,0:T(8,128)S(1)}, ...), condition=%wide.region_9.10_spmd, body=%wide.region_8.9_spmd.sunk | while | flops 403046400 | bytes 5507161 | solution.py:96
  407.9 1.9 fusion.137
  410.0 1.7 fusion.136
  411.8 1.9 fusion.137
  (107 shorter events, 52.8 us)
Async XLA Ops:
  6.5 277.9 %all-gather.5.cloned.1.call-start = ((), (), s32[]{:S(2)}) async-start(), calls=%async_computation | async-start | bytes 8912896 | tf_op jit(solution)/shard_map/all_gather | solution.py:9
  209.8 150.0 %all-gather.7.cloned.1.call-start = ((), (), s32[]{:S(2)}) async-start(), calls=%async_computation.1 | async-start | bytes 8912896 | tf_op jit(solution)/shard_map/all_gather | solution.py:9
  415.5 0.8 copy-start
Sparse Core Ops, SparseCore 0:
  209.9 74.4 all-gather.4
  286.7 73.1 all-gather.6
where the time goes:
time: 428 us; the launch traced here: 423 us
  other arithmetic  162 us (38%)
  waiting for transfers between devices  148 us (35%)
  matrix products  64.2 us (15%)
  local copies, waits for them, and re-layouts  34.6 us (8%)
  between operations  13.5 us (3%)
    another operation x8, other arithmetic, block_terms(): jax.scipy.linalg.solve_triangular(system, right, lower=True, unit_diagona...  159 us
    all_gather x2, waiting for transfers between devices, entering(): gathered = jax.tree.map(lambda a: lax.all_gather(a, axis), part)  148 us
    dot_general x16, matrix products, compose(): jnp.einsum('hve,hef->hvf', earlier[1], later[0], precision=hp) + later[1]  33.8 us
    dynamic_slice x28, local copies, waits for them, and re-layouts, one(): lax.dynamic_index_in_dim(a, hop, 0, False)  17.9 us
  transfers between devices with their start and end apart: 2, of which 2 were waited for; matrix products, arithmetic and copies ran while one was open for 0% of the time, Pallas kernels for 0%

commit v1 on v0

v1 whole, which is shorter than its diff:
```python
import functools

import jax
import jax.numpy as jnp
from jax import lax
from jax.experimental import pallas as pl
from jax.experimental.pallas import tpu as pltpu
from jax.sharding import PartitionSpec as P

F32 = jnp.float32
BF16 = jnp.bfloat16
NN = (((1,), (0,)), ((), ()))
NT = (((1,), (1,)), ((), ()))
TN = (((0,), (0,)), ((), ()))
VMEM_LIMIT = 48 * 1024 * 1024


def dot(a, b, dims=NN):
    return lax.dot_general(a, b, dims, preferred_element_type=F32)


def split(a):
    high = a.astype(BF16)
    return high, (a - high.astype(F32)).astype(BF16)


def dot2(a, b, dims=NN):
    return dot(a[0], b, dims) + dot(a[1], b, dims)


def dot3(a, b, dims=NN):
    return dot(a[0], b[0], dims) + (dot(a[0], b[1], dims) + dot(a[1], b[0], dims))


def inverse_unit_norm(field):
    return lax.rsqrt(jnp.sum(field * field, axis=-1, keepdims=True) + 1e-06)


def head_terms(q, k, v, beta):
    rows, width = k.shape
    wide_v = v.shape[1]
    rk = inverse_unit_norm(k.astype(F32))
    qf = q.astype(F32)
    rq = inverse_unit_norm(qf)
    lane = lax.broadcasted_iota(jnp.int32, (rows, 128), 1)
    packed = jnp.where(lane == 0, rk, jnp.where(lane == 1, beta, 0.0)).T
    rk_row = packed[0:1]
    beta_row = packed[1:2]
    row = lax.broadcasted_iota(jnp.int32, (rows, rows), 0)
    col = lax.broadcasted_iota(jnp.int32, (rows, rows), 1)
    lower = jnp.where(row > col, dot(k, k, NT) * (beta * rk) * rk_row, 0.0)
    scores = split(jnp.where(row >= col, dot(q, k, NT) * rq * rk_row, 0.0))
    low_h, low_l = split(lower)
    inv = jnp.where(row == col, 1.0, 0.0) - jnp.where((row >> 1) == (col >> 1), lower, 0.0)
    bit = 1
    zero = jnp.zeros((), BF16)
    while (1 << bit) < rows:
        mask = (row >> bit) == ((col >> bit) ^ 1)
        cut = (jnp.where(mask, low_h, zero), jnp.where(mask, low_l, zero))
        halves = split(inv)
        inv = inv - dot3(halves, split(dot3(cut, halves)))
        bit += 1
    inv_v = inv * beta_row
    ubar = dot2(split(inv_v), v)
    wmat = dot2(split(inv_v * rk_row), k)
    both = jnp.concatenate([ubar, wmat], axis=1)
    mixed = dot3(scores, split(both))
    local = mixed[:, :wide_v]
    fix = qf * rq - mixed[:, wide_v:]
    maps = dot2(split(both * rk), k, TN)
    eye = jnp.where(
        lax.broadcasted_iota(jnp.int32, (width, width), 0)
        == lax.broadcasted_iota(jnp.int32, (width, width), 1),
        1.0,
        0.0,
    )
    return eye - maps[wide_v:], maps[:wide_v], local, fix


def local_kernel(q_ref, k_ref, v_ref, s_ref, th_ref, tl_ref, o_ref, lo_ref, qh_ref, ql_ref, wide, qs, ks, vs):
    heads = q_ref.shape[1]
    for source, target in ((k_ref, ks), (v_ref, vs), (q_ref, qs)):
        wide[...] = source[...].astype(F32)
        for h in range(heads):
            target[h] = wide[:, h, :].astype(BF16)
    strengths = s_ref[...]
    lane = lax.broadcasted_iota(jnp.int32, strengths.shape, 1)

    def pair(step, unused):
        for half in range(2):
            h = step * 2 + half
            beta = jnp.sum(jnp.where(lane == h, strengths, 0.0), axis=1, keepdims=True)
            trans, offset, local, fix = head_terms(qs[h], ks[h], vs[h], beta)
            th_ref[h], tl_ref[h] = split(trans)
            o_ref[h] = offset
            lo_ref[h] = local
            qh_ref[h], ql_ref[h] = split(fix)
        return unused

    lax.fori_loop(0, heads // 2, pair, 0)


def chain_kernel(segs, inners, th_ref, tl_ref, o_ref, in_ref, landed, leaving, send_sem, recv_sem):
    heads = o_ref.shape[0]
    total = segs * inners
    me = lax.axis_index("seg") * inners + lax.axis_index("inner")

    def place(index):
        index = lax.rem(index + total, total)
        return {"seg": index // inners, "inner": lax.rem(index, inners)}

    barrier = pltpu.get_barrier_semaphore()
    for step in (-1, 1):
        pl.semaphore_signal(barrier, inc=1, device_id=place(me + step), device_id_type=pl.DeviceIdType.MESH)
    pl.semaphore_wait(barrier, 2)

    def hop(h):
        return pltpu.make_async_remote_copy(
            src_ref=leaving.at[h],
            dst_ref=landed.at[h],
            send_sem=send_sem.at[h],
            recv_sem=recv_sem.at[h],
            device_id=place(me + 1),
            device_id_type=pl.DeviceIdType.MESH,
        )

    for h in range(heads):

        @pl.when(me > 0)
        def _():
            hop(h).wait_recv()
            state = landed[h]
            in_ref[h] = state

            @pl.when(me < total - 1)
            def _():
                leaving[h] = o_ref[h] + dot3(split(state), (th_ref[h], tl_ref[h]))

        @pl.when(me == 0)
        def _():
            in_ref[h] = jnp.zeros_like(in_ref[h])
            leaving[h] = o_ref[h]

        @pl.when(me < total - 1)
        def _():
            hop(h).start()

    @pl.when(me < total - 1)
    def _():
        for h in range(heads):
            hop(h).wait_send()


def emit_kernel(in_ref, lo_ref, qh_ref, ql_ref, out_ref, wide):
    heads = in_ref.shape[0]
    for h in range(heads):
        wide[:, h, :] = lo_ref[h] + dot3((qh_ref[h], ql_ref[h]), split(in_ref[h]), NT)
    out_ref[...] = wide[...].astype(out_ref.dtype)


def body(segs, inners, queries, keys, values, strengths):
    rows, heads, width = queries.shape
    wide_v = values.shape[2]
    vm = pl.BlockSpec(memory_space=pltpu.VMEM)
    shape = jax.ShapeDtypeStruct
    params = pltpu.CompilerParams(vmem_limit_bytes=VMEM_LIMIT)
    th, tl, off, local, qh, ql = pl.pallas_call(
        local_kernel,
        out_shape=[
            shape((heads, width, width), BF16),
            shape((heads, width, width), BF16),
            shape((heads, wide_v, width), F32),
            shape((heads, rows, wide_v), F32),
            shape((heads, rows, width), BF16),
            shape((heads, rows, width), BF16),
        ],
        in_specs=[vm] * 4,
        out_specs=[vm] * 6,
        scratch_shapes=[
            pltpu.VMEM((rows, heads, width), F32),
            pltpu.VMEM((heads, rows, width), BF16),
            pltpu.VMEM((heads, rows, width), BF16),
            pltpu.VMEM((heads, rows, wide_v), BF16),
        ],
        compiler_params=params,
        name="local_terms",
    )(queries, keys, values, strengths)
    entering = pl.pallas_call(
        functools.partial(chain_kernel, segs, inners),
        out_shape=shape((heads, wide_v, width), F32),
        in_specs=[vm] * 3,
        out_specs=vm,
        scratch_shapes=[
            pltpu.VMEM((heads, wide_v, width), F32),
            pltpu.VMEM((heads, wide_v, width), F32),
            pltpu.SemaphoreType.DMA((heads,)),
            pltpu.SemaphoreType.DMA((heads,)),
        ],
        compiler_params=pltpu.CompilerParams(
            collective_id=0, has_side_effects=True, vmem_limit_bytes=VMEM_LIMIT
        ),
        name="state_chain",
    )(th, tl, off)
    return pl.pallas_call(
        emit_kernel,
        out_shape=shape((rows, heads, wide_v), BF16),
        in_specs=[vm] * 4,
        out_specs=vm,
        scratch_shapes=[pltpu.VMEM((rows, heads, wide_v), F32)],
        compiler_params=params,
        name="emit",
    )(entering, local, qh, ql)


def solution(mesh):
    split_rows = ("grp", "seg", "inner")
    placed = (
        P(split_rows, None, None),
        P(split_rows, None, None),
        P(split_rows, None, None),
        P(split_rows, None),
    )
    return jax.shard_map(
        functools.partial(body, mesh.shape["seg"], mesh.shape["inner"]),
        mesh=mesh,
        in_specs=placed,
        out_specs=P(split_rows, None, None),
        check_vma=False,
    )
```

time: 428 us -> 108 us (0.25)
  other arithmetic: 162 us -> 0 us
  waiting for transfers between devices: 148 us -> 0 us
  Pallas kernels: 0 us -> 103 us
  matrix products: 64.2 us -> 0 us
  local copies, waits for them, and re-layouts: 34.6 us -> 3.94 us
  between operations: 13.5 us -> 0.03 us
    another operation x12 -> x0, other arithmetic: 159 us -> none  [the longest x8 159 us: block_terms(): jax.scipy.linalg.solve_triangular(system, right, lower=True, unit_diagona...]
    all_gather x2 -> x0, waiting for transfers between devices: 148 us -> none  [entering(): gathered = jax.tree.map(lambda a: lax.all_gather(a, axis), part)]
    pallas_call x0 -> x3, Pallas kernels: none -> 103 us  [the longest x1 55.6 us: body(): pl.pallas_call(functools.partial(chain_kernel, segs, inners), out_shape=s...]
    dot_general x34 -> x0, matrix products: 59.8 us -> none  [the longest x16 33.8 us: compose(): jnp.einsum('hve,hef->hvf', earlier[1], later[0], precision=hp) + later[1]]
    dynamic_slice x32 -> x0, local copies, waits for them, and re-layouts: 22 us -> none  [the longest x28 17.9 us: one(): lax.dynamic_index_in_dim(a, hop, 0, False)]
    while x22 -> x0, local copies, waits for them, and re-layouts: 5.77 us -> none  [the longest x2 3.03 us: body(): lax.scan(fold_maps, identity, (all_trans, all_offset))]
    dynamic_update_slice x6 -> x0, local copies, waits for them, and re-layouts: 4.55 us -> none  [the longest x4 4.16 us: body(): lax.map(terms_of, (qs, ks, vs, bs))]
    another operation x2 -> x0, matrix products: 4.47 us -> none  [block_terms(): jax.scipy.linalg.solve_triangular(system, right, lower=True, unit_diagona...]
  transfers between devices with their start and end apart: 2 -> 0, of which waited for: 2 -> 0; matrix products, arithmetic and copies ran while one was open for 0% -> 0% of each run, Pallas kernels for 0% -> 0%
where the time goes in v1:
time: 108 us; the launch traced here: 107 us
  Pallas kernels  103 us (95%)
  local copies, waits for them, and re-layouts  3.94 us (4%)
    pallas_call x1, Pallas kernels, body(): pl.pallas_call(functools.partial(chain_kernel, segs, inners), out_shape=s...  55.6 us
    pallas_call x1, Pallas kernels, body(): pl.pallas_call(local_kernel, out_shape=[shape((heads, width, width), BF16...  45.8 us
    unnamed x7, local copies, waits for them, and re-layouts  3.94 us

profile of v1, /device:TPU:25, one launch (start us, length us, event | category | flops | bytes accessed | tf_op | source)
XLA Modules:
  0.0 107.2 jit_solution(10634869274465588235)
XLA Ops:
  0.0 0.8 copy.5.s_ref
  0.8 0.0 copy-start
  0.8 1.0 copy-done
  1.9 0.0 copy-start.1
  1.9 1.0 copy-done.1
  2.9 0.0 copy-start.2
  2.9 1.0 copy-done.2
  4.0 45.8 %local_terms.1 = (bf16[8,128,128]{2,1,0:T(8,128)(2,1)S(1)}, bf16[8,128,128]{2,1,0:T(8,128)(2,1)S(1)}, f32[8,128,128]{2,1,0:T(8,128)S(1)}, f32[8,256,128]{2,1,0:T...) custom-call(bf16[256,8,128]{2,1,0:T(8,128)(2,1)S(1)} %copy-done, ...), custom_call_target="tpu_custom_call" | custom-call | tf_op jit(solution)/shard_map/local_terms/pallas_call | solution.py:167
  49.8 55.6 %state_chain.1.in_ref = f32[8,128,128]{2,1,0:T(8,128)S(1)} custom-call(bf16[8,128,128]{2,1,0:T(8,128)(2,1)S(1)} %get-tuple-element.11.th_ref, bf16[8,128,128]{2,1,0:T(8,128)(2,1)S(1)} %get-tuple-element.12.tl_ref, f32[8,128,128]{2,1,0:T(8,128)S(1)} %get-tuple-element.13.o_ref), custom_call_target="tpu_custom_call" | custom-call | tf_op jit(solution)/shard_map/state_chain/pallas_call | solution.py:188
  105.4 1.9 %emit.1 = bf16[256,8,128]{2,1,0:T(8,128)(2,1)} custom-call(f32[8,128,128]{2,1,0:T(8,128)S(1)} %state_chain.1.in_ref, f32[8,256,128]{2,1,0:T(8,128)S(1)} %get-tuple-element.14.lo_ref, bf16[8,256,128]{2,1,0:T(8,128)(2,1)S(1)} %get-tuple-element.15.qh_ref, bf16[8,256,128]{2,1,0:T(8,128)(2,1)S(1)} %get-tuple-element.16.ql_ref), custom_call_target="tpu_custom_call" | custom-call | tf_op jit(solution)/shard_map/emit/pallas_call | solution.py:204
Async XLA Ops:
  0.8 1.0 copy-start
  1.9 1.0 copy-start.1
  2.9 1.0 copy-start.2

commit v2 on v1

v2 whole, which is shorter than its diff:
```python
import functools

import jax
import jax.numpy as jnp
from jax import lax
from jax.experimental import pallas as pl
from jax.experimental.pallas import tpu as pltpu
from jax.sharding import PartitionSpec as P

F32 = jnp.float32
BF16 = jnp.bfloat16
NN = (((1,), (0,)), ((), ()))
NT = (((1,), (1,)), ((), ()))
TN = (((0,), (0,)), ((), ()))
GROUP = 2
VMEM_LIMIT = 48 * 1024 * 1024


def dot(a, b, dims=NN):
    return lax.dot_general(a, b, dims, preferred_element_type=F32)


def split(a):
    high = a.astype(BF16)
    return high, (a - high.astype(F32)).astype(BF16)


def dot2(a, b, dims=NN):
    return dot(a[0], b, dims) + dot(a[1], b, dims)


def dot3(a, b, dims=NN):
    (left,), (right,) = dims[0]
    if a[0].shape[left] == 128:
        joined = dot(
            jnp.concatenate([a[0], a[1]], axis=left),
            jnp.concatenate([b[0], b[0]], axis=right),
            dims,
        )
        return joined + dot(a[0], b[1], dims)
    return dot(a[0], b[0], dims) + (dot(a[0], b[1], dims) + dot(a[1], b[0], dims))


def inverse_unit_norm(field):
    return lax.rsqrt(jnp.sum(field * field, axis=-1, keepdims=True) + 1e-06)


def iotas(rows):
    return (
        lax.broadcasted_iota(jnp.int32, (rows, rows), 0),
        lax.broadcasted_iota(jnp.int32, (rows, rows), 1),
    )


def unit_lower_inverses(blocks):
    rows = blocks[0].shape[0]
    row, col = iotas(rows)
    eye = jnp.where(row == col, 1.0, 0.0)
    first = (row >> 1) == (col >> 1)
    inverses = [eye - jnp.where(first, n, 0.0) for n in blocks]
    lowers = [split(n) for n in blocks]
    bit = 1
    while (1 << bit) < rows:
        mask = (row >> bit) == ((col >> bit) ^ 1)
        halves = [split(x) for x in inverses]
        right = [split(dot3(n, x)) for n, x in zip(lowers, halves)]
        whole = [dot3(x, y) for x, y in zip(halves, right)]
        inverses = [x - jnp.where(mask, w, 0.0) for x, w in zip(inverses, whole)]
        bit += 1
    return inverses


def group_terms(group):
    rows, width = group[0][1].shape
    wide_v = group[0][2].shape[1]
    half = rows // 2
    row, col = iotas(rows)
    lane = lax.broadcasted_iota(jnp.int32, (rows, 128), 1)
    lowers, sides, blocks = [], [], []
    for q, k, v, beta in group:
        rk = inverse_unit_norm(k.astype(F32))
        packed = jnp.where(lane == 0, rk, jnp.where(lane == 1, beta, 0.0)).T
        lower = jnp.where(row > col, dot(k, k, NT) * (beta * rk) * packed[0:1], 0.0)
        lowers.append(lower)
        sides.append((rk, packed[0:1], packed[1:2]))
        blocks += [lower[:half, :half], lower[half:, half:]]
    diagonal = unit_lower_inverses(blocks)
    halves = [split(x) for x in diagonal]
    corners = [
        split(dot3(split(n[half:, :half]), halves[2 * i])) for i, n in enumerate(lowers)
    ]
    corners = [dot3(halves[2 * i + 1], c) for i, c in enumerate(corners)]
    zero = jnp.zeros((half, half), F32)
    inverses = [
        jnp.concatenate(
            [
                jnp.concatenate([diagonal[2 * i], zero], axis=1),
                jnp.concatenate([-c, diagonal[2 * i + 1]], axis=1),
            ],
            axis=0,
        )
        for i, c in enumerate(corners)
    ]
    eye = jnp.where(iotas(width)[0] == iotas(width)[1], 1.0, 0.0)
    results = []
    for (q, k, v, beta), (rk, rk_row, beta_row), inv in zip(group, sides, inverses):
        inv_v = inv * beta_row
        ubar = dot2(split(inv_v), v)
        wmat = dot2(split(inv_v * rk_row), k)
        both = jnp.concatenate([ubar, wmat], axis=1)
        maps = dot2(split(both * rk), k, TN)
        results.append((eye - maps[wide_v:], maps[:wide_v], both, rk_row))
    return results


def query_terms(q, k, both, rk_row):
    rows = q.shape[0]
    wide_v = both.shape[1] - k.shape[1]
    row, col = iotas(rows)
    qf = q.astype(F32)
    rq = inverse_unit_norm(qf)
    scores = jnp.where(row >= col, dot(q, k, NT) * rq * rk_row, 0.0)
    mixed = dot3(split(scores), split(both))
    return mixed[:, :wide_v], qf * rq - mixed[:, wide_v:]


def maps_kernel(
    segs, inners, q_ref, k_ref, v_ref, s_ref, in_ref, lo_ref, qh_ref, ql_ref,
    wide, qs, ks, vs, own, earlier, pair, landed, leaving,
    map_send, map_recv, next_send, fan_send, state_recv,
):
    heads = q_ref.shape[1]
    wide_k = own.shape[2]
    total = segs * inners
    me = lax.axis_index("seg") * inners + lax.axis_index("inner")
    odd = lax.rem(me, 2) == 1
    even = lax.rem(me, 2) == 0
    first = me < 2
    last = me >= total - 2

    def place(index):
        index = lax.rem(index + total, total)
        return {"seg": index // inners, "inner": lax.rem(index, inners)}

    barrier = pltpu.get_barrier_semaphore()
    for step in (-2, -1, 1, 2):
        pl.semaphore_signal(barrier, inc=1, device_id=place(me + step), device_id_type=pl.DeviceIdType.MESH)

    def send(source, target, send_sem, recv_sem, h, step):
        return pltpu.make_async_remote_copy(
            src_ref=source.at[h],
            dst_ref=target.at[h],
            send_sem=send_sem.at[h],
            recv_sem=recv_sem.at[h],
            device_id=place(me + step),
            device_id_type=pl.DeviceIdType.MESH,
        )

    def map_hop(h):
        return send(own, earlier, map_send, map_recv, h, 1)

    def next_hop(h):
        return send(leaving, landed, next_send, state_recv, h, 2)

    def fan_hop(h):
        return send(leaving, landed, fan_send, state_recv, h, 1)

    for source, target in ((k_ref, ks), (v_ref, vs), (q_ref, qs)):
        wide[...] = source[...].astype(F32)
        for h in range(heads):
            target[h] = wide[:, h, :].astype(BF16)
    strengths = s_ref[...]
    lane = lax.broadcasted_iota(jnp.int32, strengths.shape, 1)
    pl.semaphore_wait(barrier, 4)

    def local(step, unused):
        places = [step * GROUP + i for i in range(GROUP)]
        group = []
        for h in places:
            beta = jnp.sum(jnp.where(lane == h, strengths, 0.0), axis=1, keepdims=True)
            group.append((qs[h], ks[h], vs[h], beta))
        terms = group_terms(group)
        for h, (trans, offset, both, rk_row) in zip(places, terms):
            own[h, :wide_k, :] = trans
            own[h, wide_k:, :] = offset

        @pl.when(even)
        def _():
            for h in places:
                map_hop(h).start()

        for h, (q, k, v, beta), (trans, offset, both, rk_row) in zip(places, group, terms):
            lo_ref[h], fix = query_terms(q, k, both, rk_row)
            qh_ref[h], ql_ref[h] = split(fix)
        return unused

    lax.fori_loop(0, heads // GROUP, local, 0)

    @pl.when(odd)
    def _():
        def compose(h, unused):
            map_hop(h).wait_recv()
            both = dot3(split(earlier[h]), split(own[h, :wide_k, :]))
            pair[h, :wide_k, :] = both[:wide_k]
            pair[h, wide_k:, :] = both[wide_k:] + own[h, wide_k:, :]
            return unused

        def advance(h, unused):
            @pl.when(first)
            def _():
                landed[h] = jnp.zeros_like(landed[h])

            @pl.when(jnp.logical_not(first))
            def _():
                next_hop(h).wait_recv()

            state = split(landed[h])

            @pl.when(jnp.logical_not(last))
            def _():
                leaving[h] = dot3(state, split(pair[h, :wide_k, :])) + pair[h, wide_k:, :]
                next_hop(h).start()
                fan_hop(h).start()

            in_ref[h] = dot3(state, split(earlier[h, :wide_k, :])) + earlier[h, wide_k:, :]
            return unused

        lax.fori_loop(0, heads, compose, 0)
        lax.fori_loop(0, heads, advance, 0)

        @pl.when(jnp.logical_not(last))
        def _():
            for h in range(heads):
                next_hop(h).wait_send()
                fan_hop(h).wait_send()

    @pl.when(even)
    def _():
        for h in range(heads):
            map_hop(h).wait_send()

        @pl.when(first)
        def _():
            in_ref[...] = jnp.zeros_like(in_ref)

        @pl.when(jnp.logical_not(first))
        def _():
            for h in range(heads):
                fan_hop(h).wait_recv()
            in_ref[...] = landed[...]


def emit_kernel(in_ref, lo_ref, qh_ref, ql_ref, out_ref, wide):
    heads = in_ref.shape[0]
    for h in range(heads):
        wide[:, h, :] = lo_ref[h] + dot3((qh_ref[h], ql_ref[h]), split(in_ref[h]), NT)
    out_ref[...] = wide[...].astype(out_ref.dtype)


def body(segs, inners, queries, keys, values, strengths):
    rows, heads, width = queries.shape
    wide_v = values.shape[2]
    vm = pl.BlockSpec(memory_space=pltpu.VMEM)
    shape = jax.ShapeDtypeStruct
    params = pltpu.CompilerParams(vmem_limit_bytes=VMEM_LIMIT)
    dma = pltpu.SemaphoreType.DMA((heads,))
    maps = pltpu.VMEM((heads, width + wide_v, width), F32)
    states = pltpu.VMEM((heads, wide_v, width), F32)
    entering, local, qh, ql = pl.pallas_call(
        functools.partial(maps_kernel, segs, inners),
        out_shape=[
            shape((heads, wide_v, width), F32),
            shape((heads, rows, wide_v), F32),
            shape((heads, rows, width), BF16),
            shape((heads, rows, width), BF16),
        ],
        in_specs=[vm] * 4,
        out_specs=[vm] * 4,
        scratch_shapes=[
            pltpu.VMEM((rows, heads, width), F32),
            pltpu.VMEM((heads, rows, width), BF16),
            pltpu.VMEM((heads, rows, width), BF16),
            pltpu.VMEM((heads, rows, wide_v), BF16),
            maps, maps, maps, states, states,
            dma, dma, dma, dma, dma,
        ],
        compiler_params=pltpu.CompilerParams(
            collective_id=0, has_side_effects=True, vmem_limit_bytes=VMEM_LIMIT
        ),
        name="maps_and_chain",
    )(queries, keys, values, strengths)
    return pl.pallas_call(
        emit_kernel,
        out_shape=shape((rows, heads, wide_v), BF16),
        in_specs=[vm] * 4,
        out_specs=vm,
        scratch_shapes=[pltpu.VMEM((rows, heads, wide_v), F32)],
        compiler_params=params,
        name="emit",
    )(entering, local, qh, ql)


def solution(mesh):
    split_rows = ("grp", "seg", "inner")
    placed = (
        P(split_rows, None, None),
        P(split_rows, None, None),
        P(split_rows, None, None),
        P(split_rows, None),
    )
    return jax.shard_map(
        functools.partial(body, mesh.shape["seg"], mesh.shape["inner"]),
        mesh=mesh,
        in_specs=placed,
        out_specs=P(split_rows, None, None),
        check_vma=False,
    )
```

time: 108 us -> 71.1 us (0.66)
  Pallas kernels: 103 us -> 66.9 us
    pallas_call x2 -> x1, Pallas kernels: 101 us -> 65 us  [body(): pl.pallas_call(functools.partial(maps_kernel, segs, inners), out_shape=[s...]
where the time goes in v2:
time: 71.1 us; the launch traced here: 70.8 us
  Pallas kernels  66.9 us (94%)
  local copies, waits for them, and re-layouts  3.94 us (6%)
    pallas_call x1, Pallas kernels, body(): pl.pallas_call(functools.partial(maps_kernel, segs, inners), out_shape=[s...  65 us
    unnamed x7, local copies, waits for them, and re-layouts  3.94 us
    pallas_call x1, Pallas kernels, body(): pl.pallas_call(emit_kernel, out_shape=shape((rows, heads, wide_v), BF16),...  1.82 us

profile of v2, /device:TPU:25, one launch (start us, length us, event | category | flops | bytes accessed | tf_op | source)
XLA Modules:
  0.0 70.8 jit_solution(10500266025541642748)
XLA Ops:
  0.0 0.8 %copy.5.s_ref = f32[256,8]{1,0:T(8,128)S(1)} copy(f32[256,8]{0,1:T(8,128)} %param.7) | data formatting | bytes 16384 | tf_op args[3]
  0.8 0.0 copy-start
  0.8 1.0 %copy-done = bf16[256,8,128]{2,1,0:T(8,128)(2,1)S(1)} copy-done((bf16[256,8,128]{2,1,0:T(8,128)(2,1)S(1)}, bf16[256,8,128]{2,1,0:T(8,128)(2,1)}, u32[]{:S(2)}) %copy-start) | copy-done | bytes 524312
  1.9 0.0 copy-start.1
  1.9 1.0 %copy-done.1 = bf16[256,8,128]{2,1,0:T(8,128)(2,1)S(1)} copy-done((bf16[256,8,128]{2,1,0:T(8,128)(2,1)S(1)}, bf16[256,8,128]{2,1,0:T(8,128)(2,1)}, u32[]{:S(2)}) %copy-start.1) | copy-done | bytes 524312
  2.9 0.0 copy-start.2
  2.9 1.0 %copy-done.2 = bf16[256,8,128]{2,1,0:T(8,128)(2,1)S(1)} copy-done((bf16[256,8,128]{2,1,0:T(8,128)(2,1)S(1)}, bf16[256,8,128]{2,1,0:T(8,128)(2,1)}, u32[]{:S(2)}) %copy-start.2) | copy-done | bytes 524312
  4.0 65.0 %maps_and_chain.1 = (f32[8,128,128]{2,1,0:T(8,128)S(1)}, f32[8,256,128]{2,1,0:T(8,128)S(1)}, bf16[8,256,128]{2,1,0:T(8,128)(2,1)S(1)}, bf16[8,256,128]{2,1,0:T(8,128)(2,1)S(1)}) custom-call(bf16[256,8,128]{2,1,0:T(8,128)(2,1)S(1)} %copy-done, bf16[256,8,128]{2,1,0:T(8,128)(2,1)S(1)} %copy-done.1, bf16[256,8,128]{2,1,0:T(8,128)(2,1)S(1)} %copy-done.2, ...), custom_call_target="tpu_custom_call" | custom-call | tf_op jit(solution)/shard_map/maps_and_chain/pallas_call | solution.py:269
  69.0 1.8 %emit.1 = bf16[256,8,128]{2,1,0:T(8,128)(2,1)} custom-call(f32[8,128,128]{2,1,0:T(8,128)S(1)} %get-tuple-element.9.in_ref, f32[8,256,128]{2,1,0:T(8,128)S(1)} %get-tuple-element.10.lo_ref, bf16[8,256,128]{2,1,0:T(8,128)(2,1)S(1)} %get-tuple-element.11.qh_ref, bf16[8,256,128]{2,1,0:T(8,128)(2,1)S(1)} %get-tuple-element.12.ql_ref), custom_call_target="tpu_custom_call" | custom-call | tf_op jit(solution)/shard_map/emit/pallas_call | solution.py:292
Async XLA Ops:
  0.8 1.0 %copy-start = (bf16[256,8,128]{2,1,0:T(8,128)(2,1)S(1)}, bf16[256,8,128]{2,1,0:T(8,128)(2,1)}, u32[]{:S(2)}) copy-start(bf16[256,8,128]{2,1,0:T(8,128)(2,1)} %q_ref.1) | copy-start | bytes 1572868
  1.9 1.0 %copy-start.1 = (bf16[256,8,128]{2,1,0:T(8,128)(2,1)S(1)}, bf16[256,8,128]{2,1,0:T(8,128)(2,1)}, u32[]{:S(2)}) copy-start(bf16[256,8,128]{2,1,0:T(8,128)(2,1)} %k_ref.1) | copy-start | bytes 1572868
  2.9 1.0 %copy-start.2 = (bf16[256,8,128]{2,1,0:T(8,128)(2,1)S(1)}, bf16[256,8,128]{2,1,0:T(8,128)(2,1)}, u32[]{:S(2)}) copy-start(bf16[256,8,128]{2,1,0:T(8,128)(2,1)} %v_ref.1) | copy-start | bytes 1572868

commit v3 on v2

--- a/solution.py
+++ b/solution.py
@@ -126,7 +126,7 @@
 
 def maps_kernel(
     segs, inners, q_ref, k_ref, v_ref, s_ref, in_ref, lo_ref, qh_ref, ql_ref,
-    wide, qs, ks, vs, own, earlier, pair, landed, leaving,
+    wide, qs, ks, vs, solved, scale, own, earlier, pair_h, pair_l, pair_o, landed, leaving,
     map_send, map_recv, next_send, fan_send, state_recv,
 ):
     heads = q_ref.shape[1]
@@ -163,7 +163,7 @@
         return send(leaving, landed, next_send, state_recv, h, 2)
 
     def fan_hop(h):
-        return send(leaving, landed, fan_send, state_recv, h, 1)
+        return send(landed, landed, fan_send, state_recv, h, -1)
 
     for source, target in ((k_ref, ks), (v_ref, vs), (q_ref, qs)):
         wide[...] = source[...].astype(F32)
@@ -183,56 +183,95 @@
         for h, (trans, offset, both, rk_row) in zip(places, terms):
             own[h, :wide_k, :] = trans
             own[h, wide_k:, :] = offset
+            solved[h] = both
+            scale[h] = jnp.broadcast_to(rk_row, scale.shape[1:])
 
         @pl.when(even)
         def _():
             for h in places:
                 map_hop(h).start()
 
-        for h, (q, k, v, beta), (trans, offset, both, rk_row) in zip(places, group, terms):
-            lo_ref[h], fix = query_terms(q, k, both, rk_row)
+        return unused
+
+    lax.fori_loop(0, heads // GROUP, local, 0)
+
+    def query_side(step, unused):
+        for i in range(GROUP):
+            h = step * GROUP + i
+            lo_ref[h], fix = query_terms(qs[h], ks[h], solved[h], scale[h, 0:1, :])
             qh_ref[h], ql_ref[h] = split(fix)
         return unused
 
-    lax.fori_loop(0, heads // GROUP, local, 0)
+    early = jnp.logical_and(odd, me < total // 2)
+
+    @pl.when(jnp.logical_not(early))
+    def _():
+        lax.fori_loop(0, heads // GROUP, query_side, 0)
+
+    def enter(h):
+        in_ref[h] = dot3(split(landed[h]), split(earlier[h, :wide_k, :])) + earlier[h, wide_k:, :]
 
     @pl.when(odd)
     def _():
-        def compose(h, unused):
+        for h in range(heads):
             map_hop(h).wait_recv()
-            both = dot3(split(earlier[h]), split(own[h, :wide_k, :]))
-            pair[h, :wide_k, :] = both[:wide_k]
-            pair[h, wide_k:, :] = both[wide_k:] + own[h, wide_k:, :]
-            return unused
-
-        def advance(h, unused):
+            later = split(own[h, :wide_k, :])
+
             @pl.when(first)
             def _():
-                landed[h] = jnp.zeros_like(landed[h])
+                offset = dot3(split(earlier[h, wide_k:, :]), later)
+                leaving[h] = offset + own[h, wide_k:, :]
+                next_hop(h).start()
 
             @pl.when(jnp.logical_not(first))
             def _():
-                next_hop(h).wait_recv()
-
-            state = split(landed[h])
+                both = dot3(split(earlier[h]), later)
+                pair_h[h], pair_l[h] = split(both[:wide_k])
+                pair_o[h] = both[wide_k:] + own[h, wide_k:, :]
+
+        def advance(h, unused):
+            next_hop(h).wait_recv()
 
             @pl.when(jnp.logical_not(last))
             def _():
-                leaving[h] = dot3(state, split(pair[h, :wide_k, :])) + pair[h, wide_k:, :]
+                leaving[h] = dot3(split(landed[h]), (pair_h[h], pair_l[h])) + pair_o[h]
                 next_hop(h).start()
-                fan_hop(h).start()
-
-            in_ref[h] = dot3(state, split(earlier[h, :wide_k, :])) + earlier[h, wide_k:, :]
+
+            fan_hop(h).start()
+
+            @pl.when(last)
+            def _():
+                enter(h)
+
             return unused
 
-        lax.fori_loop(0, heads, compose, 0)
-        lax.fori_loop(0, heads, advance, 0)
-
-        @pl.when(jnp.logical_not(last))
+        @pl.when(first)
         def _():
             for h in range(heads):
-                next_hop(h).wait_send()
-                fan_hop(h).wait_send()
+                in_ref[h] = earlier[h, wide_k:, :]
+
+        @pl.when(jnp.logical_not(first))
+        def _():
+            lax.fori_loop(0, heads, advance, 0)
+
+        @pl.when(jnp.logical_not(jnp.logical_or(first, last)))
+        def _():
+            for h in range(heads):
+                enter(h)
+
+    @pl.when(early)
+    def _():
+        lax.fori_loop(0, heads // GROUP, query_side, 0)
+
+    @pl.when(jnp.logical_and(odd, jnp.logical_not(last)))
+    def _():
+        for h in range(heads):
+            next_hop(h).wait_send()
+
+    @pl.when(jnp.logical_and(odd, jnp.logical_not(first)))
+    def _():
+        for h in range(heads):
+            fan_hop(h).wait_send()
 
     @pl.when(even)
     def _():
@@ -265,6 +304,7 @@
     params = pltpu.CompilerParams(vmem_limit_bytes=VMEM_LIMIT)
     dma = pltpu.SemaphoreType.DMA((heads,))
     maps = pltpu.VMEM((heads, width + wide_v, width), F32)
+    halves = pltpu.VMEM((heads, width, width), BF16)
     states = pltpu.VMEM((heads, wide_v, width), F32)
     entering, local, qh, ql = pl.pallas_call(
         functools.partial(maps_kernel, segs, inners),
@@ -281,7 +321,9 @@
             pltpu.VMEM((heads, rows, width), BF16),
             pltpu.VMEM((heads, rows, width), BF16),
             pltpu.VMEM((heads, rows, wide_v), BF16),
-            maps, maps, maps, states, states,
+            pltpu.VMEM((heads, rows, wide_v + width), F32),
+            pltpu.VMEM((heads, 8, rows), F32),
+            maps, maps, halves, halves, states, states, states,
             dma, dma, dma, dma, dma,
         ],
         compiler_params=pltpu.CompilerParams(

time: 71.1 us -> 63.8 us (0.90)
  Pallas kernels: 66.9 us -> 59.5 us
    pallas_call x1, Pallas kernels: 65 us -> 57.7 us  [body(): pl.pallas_call(functools.partial(maps_kernel, segs, inners), out_shape=[s...]
where the time goes in v3:
time: 63.8 us; the launch traced here: 63.5 us
  Pallas kernels  59.5 us (93%)
  local copies, waits for them, and re-layouts  3.94 us (6%)
    pallas_call x1, Pallas kernels, body(): pl.pallas_call(functools.partial(maps_kernel, segs, inners), out_shape=[s...  57.7 us
    unnamed x7, local copies, waits for them, and re-layouts  3.94 us
    pallas_call x1, Pallas kernels, body(): pl.pallas_call(emit_kernel, out_shape=shape((rows, heads, wide_v), BF16),...  1.83 us

profile of v3, /device:TPU:25, one launch (start us, length us, event | category | flops | bytes accessed | tf_op | source)
XLA Modules:
  0.0 63.5 jit_solution(7676605313288419021)
XLA Ops:
  0.0 0.8 %copy.5.s_ref = f32[256,8]{1,0:T(8,128)S(1)} copy(f32[256,8]{0,1:T(8,128)} %param.7) | data formatting | bytes 16384 | tf_op args[3]
  0.8 0.0 copy-start
  0.8 1.0 %copy-done = bf16[256,8,128]{2,1,0:T(8,128)(2,1)S(1)} copy-done((bf16[256,8,128]{2,1,0:T(8,128)(2,1)S(1)}, bf16[256,8,128]{2,1,0:T(8,128)(2,1)}, u32[]{:S(2)}) %copy-start) | copy-done | bytes 524312
  1.9 0.0 copy-start.1
  1.9 1.0 %copy-done.1 = bf16[256,8,128]{2,1,0:T(8,128)(2,1)S(1)} copy-done((bf16[256,8,128]{2,1,0:T(8,128)(2,1)S(1)}, bf16[256,8,128]{2,1,0:T(8,128)(2,1)}, u32[]{:S(2)}) %copy-start.1) | copy-done | bytes 524312
  2.9 0.0 copy-start.2
  2.9 1.0 %copy-done.2 = bf16[256,8,128]{2,1,0:T(8,128)(2,1)S(1)} copy-done((bf16[256,8,128]{2,1,0:T(8,128)(2,1)S(1)}, bf16[256,8,128]{2,1,0:T(8,128)(2,1)}, u32[]{:S(2)}) %copy-start.2) | copy-done | bytes 524312
  4.0 57.7 %maps_and_chain.1 = (f32[8,128,128]{2,1,0:T(8,128)S(1)}, f32[8,256,128]{2,1,0:T(8,128)S(1)}, bf16[8,256,128]{2,1,0:T(8,128)(2,1)S(1)}, bf16[8,256,128]{2,1,0:T(8,128)(2,1)S(1)}) custom-call(bf16[256,8,128]{2,1,0:T(8,128)(2,1)S(1)} %copy-done, bf16[256,8,128]{2,1,0:T(8,128)(2,1)S(1)} %copy-done.1, bf16[256,8,128]{2,1,0:T(8,128)(2,1)S(1)} %copy-done.2, ...), custom_call_target="tpu_custom_call" | custom-call | tf_op jit(solution)/shard_map/maps_and_chain/pallas_call | solution.py:309
  61.6 1.8 %emit.1 = bf16[256,8,128]{2,1,0:T(8,128)(2,1)} custom-call(f32[8,128,128]{2,1,0:T(8,128)S(1)} %get-tuple-element.9.in_ref, f32[8,256,128]{2,1,0:T(8,128)S(1)} %get-tuple-element.10.lo_ref, bf16[8,256,128]{2,1,0:T(8,128)(2,1)S(1)} %get-tuple-element.11.qh_ref, bf16[8,256,128]{2,1,0:T(8,128)(2,1)S(1)} %get-tuple-element.12.ql_ref), custom_call_target="tpu_custom_call" | custom-call | tf_op jit(solution)/shard_map/emit/pallas_call | solution.py:334
Async XLA Ops:
  0.8 1.0 %copy-start = (bf16[256,8,128]{2,1,0:T(8,128)(2,1)S(1)}, bf16[256,8,128]{2,1,0:T(8,128)(2,1)}, u32[]{:S(2)}) copy-start(bf16[256,8,128]{2,1,0:T(8,128)(2,1)} %q_ref.1) | copy-start | bytes 1572868
  1.9 1.0 %copy-start.1 = (bf16[256,8,128]{2,1,0:T(8,128)(2,1)S(1)}, bf16[256,8,128]{2,1,0:T(8,128)(2,1)}, u32[]{:S(2)}) copy-start(bf16[256,8,128]{2,1,0:T(8,128)(2,1)} %k_ref.1) | copy-start | bytes 1572868
  2.9 1.0 %copy-start.2 = (bf16[256,8,128]{2,1,0:T(8,128)(2,1)S(1)}, bf16[256,8,128]{2,1,0:T(8,128)(2,1)}, u32[]{:S(2)}) copy-start(bf16[256,8,128]{2,1,0:T(8,128)(2,1)} %v_ref.1) | copy-start | bytes 1572868

commit v4 on v3

--- a/solution.py
+++ b/solution.py
@@ -12,7 +12,7 @@
 NN = (((1,), (0,)), ((), ()))
 NT = (((1,), (1,)), ((), ()))
 TN = (((0,), (0,)), ((), ()))
-GROUP = 2
+GROUP = 4
 VMEM_LIMIT = 48 * 1024 * 1024
 
 

time: 63.8 us -> 65 us (1.019)
  Pallas kernels: 59.5 us -> 60.8 us
    pallas_call x1, Pallas kernels: 57.7 us -> 58.9 us  [body(): pl.pallas_call(functools.partial(maps_kernel, segs, inners), out_shape=[s...]
where the time goes in v4:
time: 65 us; the launch traced here: 64.7 us
  Pallas kernels  60.8 us (94%)
  local copies, waits for them, and re-layouts  3.94 us (6%)
    pallas_call x1, Pallas kernels, body(): pl.pallas_call(functools.partial(maps_kernel, segs, inners), out_shape=[s...  58.9 us
    unnamed x7, local copies, waits for them, and re-layouts  3.94 us
    pallas_call x1, Pallas kernels, body(): pl.pallas_call(emit_kernel, out_shape=shape((rows, heads, wide_v), BF16),...  1.83 us

profile of v4, /device:TPU:25, one launch (start us, length us, event | category | flops | bytes accessed | tf_op | source)
XLA Modules:
  0.0 64.7 jit_solution(11525523923603773890)
XLA Ops:
  0.0 0.8 %copy.5.s_ref = f32[256,8]{1,0:T(8,128)S(1)} copy(f32[256,8]{0,1:T(8,128)} %param.7) | data formatting | bytes 16384 | tf_op args[3]
  0.8 0.0 copy-start
  0.8 1.0 %copy-done = bf16[256,8,128]{2,1,0:T(8,128)(2,1)S(1)} copy-done((bf16[256,8,128]{2,1,0:T(8,128)(2,1)S(1)}, bf16[256,8,128]{2,1,0:T(8,128)(2,1)}, u32[]{:S(2)}) %copy-start) | copy-done | bytes 524312
  1.9 0.0 copy-start.1
  1.9 1.0 %copy-done.1 = bf16[256,8,128]{2,1,0:T(8,128)(2,1)S(1)} copy-done((bf16[256,8,128]{2,1,0:T(8,128)(2,1)S(1)}, bf16[256,8,128]{2,1,0:T(8,128)(2,1)}, u32[]{:S(2)}) %copy-start.1) | copy-done | bytes 524312
  2.9 0.0 copy-start.2
  2.9 1.0 %copy-done.2 = bf16[256,8,128]{2,1,0:T(8,128)(2,1)S(1)} copy-done((bf16[256,8,128]{2,1,0:T(8,128)(2,1)S(1)}, bf16[256,8,128]{2,1,0:T(8,128)(2,1)}, u32[]{:S(2)}) %copy-start.2) | copy-done | bytes 524312
  4.0 58.9 %maps_and_chain.1 = (f32[8,128,128]{2,1,0:T(8,128)S(1)}, f32[8,256,128]{2,1,0:T(8,128)S(1)}, bf16[8,256,128]{2,1,0:T(8,128)(2,1)S(1)}, bf16[8,256,128]{2,1,0:T(8,128)(2,1)S(1)}) custom-call(bf16[256,8,128]{2,1,0:T(8,128)(2,1)S(1)} %copy-done, bf16[256,8,128]{2,1,0:T(8,128)(2,1)S(1)} %copy-done.1, bf16[256,8,128]{2,1,0:T(8,128)(2,1)S(1)} %copy-done.2, ...), custom_call_target="tpu_custom_call" | custom-call | tf_op jit(solution)/shard_map/maps_and_chain/pallas_call | solution.py:309
  62.9 1.8 %emit.1 = bf16[256,8,128]{2,1,0:T(8,128)(2,1)} custom-call(f32[8,128,128]{2,1,0:T(8,128)S(1)} %get-tuple-element.9.in_ref, f32[8,256,128]{2,1,0:T(8,128)S(1)} %get-tuple-element.10.lo_ref, bf16[8,256,128]{2,1,0:T(8,128)(2,1)S(1)} %get-tuple-element.11.qh_ref, bf16[8,256,128]{2,1,0:T(8,128)(2,1)S(1)} %get-tuple-element.12.ql_ref), custom_call_target="tpu_custom_call" | custom-call | tf_op jit(solution)/shard_map/emit/pallas_call | solution.py:334
Async XLA Ops:
  0.8 1.0 %copy-start = (bf16[256,8,128]{2,1,0:T(8,128)(2,1)S(1)}, bf16[256,8,128]{2,1,0:T(8,128)(2,1)}, u32[]{:S(2)}) copy-start(bf16[256,8,128]{2,1,0:T(8,128)(2,1)} %q_ref.1) | copy-start | bytes 1572868
  1.9 1.0 %copy-start.1 = (bf16[256,8,128]{2,1,0:T(8,128)(2,1)S(1)}, bf16[256,8,128]{2,1,0:T(8,128)(2,1)}, u32[]{:S(2)}) copy-start(bf16[256,8,128]{2,1,0:T(8,128)(2,1)} %k_ref.1) | copy-start | bytes 1572868
  2.9 1.0 %copy-start.2 = (bf16[256,8,128]{2,1,0:T(8,128)(2,1)S(1)}, bf16[256,8,128]{2,1,0:T(8,128)(2,1)}, u32[]{:S(2)}) copy-start(bf16[256,8,128]{2,1,0:T(8,128)(2,1)} %v_ref.1) | copy-start | bytes 1572868

commit v5 on v3

--- a/solution.py
+++ b/solution.py
@@ -186,7 +186,7 @@
             solved[h] = both
             scale[h] = jnp.broadcast_to(rk_row, scale.shape[1:])
 
-        @pl.when(even)
+        @pl.when(jnp.logical_and(even, jnp.logical_or(me < total // 2, step < heads // GROUP - 1)))
         def _():
             for h in places:
                 map_hop(h).start()
@@ -208,12 +208,17 @@
     def _():
         lax.fori_loop(0, heads // GROUP, query_side, 0)
 
+    @pl.when(jnp.logical_and(even, me >= total // 2))
+    def _():
+        for h in range(heads - GROUP, heads):
+            map_hop(h).start()
+
     def enter(h):
         in_ref[h] = dot3(split(landed[h]), split(earlier[h, :wide_k, :])) + earlier[h, wide_k:, :]
 
     @pl.when(odd)
     def _():
-        for h in range(heads):
+        def compose(h):
             map_hop(h).wait_recv()
             later = split(own[h, :wide_k, :])
 
@@ -245,14 +250,18 @@
 
             return unused
 
+        for low, high in ((0, heads - GROUP), (heads - GROUP, heads)):
+            for h in range(low, high):
+                compose(h)
+
+            @pl.when(jnp.logical_not(first))
+            def _():
+                lax.fori_loop(low, high, advance, 0)
+
         @pl.when(first)
         def _():
             for h in range(heads):
                 in_ref[h] = earlier[h, wide_k:, :]
-
-        @pl.when(jnp.logical_not(first))
-        def _():
-            lax.fori_loop(0, heads, advance, 0)
 
         @pl.when(jnp.logical_not(jnp.logical_or(first, last)))
         def _():

time: 63.8 us -> 62.2 us (0.975)
  Pallas kernels: 59.5 us -> 57.9 us
    pallas_call x1, Pallas kernels: 57.7 us -> 56 us  [body(): pl.pallas_call(functools.partial(maps_kernel, segs, inners), out_shape=[s...]
where the time goes in v5:
time: 62.2 us; the launch traced here: 61.8 us
  Pallas kernels  57.9 us (93%)
  local copies, waits for them, and re-layouts  3.94 us (6%)
    pallas_call x1, Pallas kernels, body(): pl.pallas_call(functools.partial(maps_kernel, segs, inners), out_shape=[s...  56 us
    unnamed x7, local copies, waits for them, and re-layouts  3.94 us
    pallas_call x1, Pallas kernels, body(): pl.pallas_call(emit_kernel, out_shape=shape((rows, heads, wide_v), BF16),...  1.82 us

profile of v5, /device:TPU:25, one launch (start us, length us, event | category | flops | bytes accessed | tf_op | source)
XLA Modules:
  0.0 61.8 jit_solution(7984229894754489631)
XLA Ops:
  0.0 0.8 %copy.5.s_ref = f32[256,8]{1,0:T(8,128)S(1)} copy(f32[256,8]{0,1:T(8,128)} %param.7) | data formatting | bytes 16384 | tf_op args[3]
  0.8 0.0 copy-start
  0.8 1.0 %copy-done = bf16[256,8,128]{2,1,0:T(8,128)(2,1)S(1)} copy-done((bf16[256,8,128]{2,1,0:T(8,128)(2,1)S(1)}, bf16[256,8,128]{2,1,0:T(8,128)(2,1)}, u32[]{:S(2)}) %copy-start) | copy-done | bytes 524312
  1.9 0.0 copy-start.1
  1.9 1.0 %copy-done.1 = bf16[256,8,128]{2,1,0:T(8,128)(2,1)S(1)} copy-done((bf16[256,8,128]{2,1,0:T(8,128)(2,1)S(1)}, bf16[256,8,128]{2,1,0:T(8,128)(2,1)}, u32[]{:S(2)}) %copy-start.1) | copy-done | bytes 524312
  2.9 0.0 copy-start.2
  2.9 1.0 %copy-done.2 = bf16[256,8,128]{2,1,0:T(8,128)(2,1)S(1)} copy-done((bf16[256,8,128]{2,1,0:T(8,128)(2,1)S(1)}, bf16[256,8,128]{2,1,0:T(8,128)(2,1)}, u32[]{:S(2)}) %copy-start.2) | copy-done | bytes 524312
  4.0 56.0 %maps_and_chain.1 = (f32[8,128,128]{2,1,0:T(8,128)S(1)}, f32[8,256,128]{2,1,0:T(8,128)S(1)}, bf16[8,256,128]{2,1,0:T(8,128)(2,1)S(1)}, bf16[8,256,128]{2,1,0:T(8,128)(2,1)S(1)}) custom-call(bf16[256,8,128]{2,1,0:T(8,128)(2,1)S(1)} %copy-done, bf16[256,8,128]{2,1,0:T(8,128)(2,1)S(1)} %copy-done.1, bf16[256,8,128]{2,1,0:T(8,128)(2,1)S(1)} %copy-done.2, ...), custom_call_target="tpu_custom_call" | custom-call | tf_op jit(solution)/shard_map/maps_and_chain/pallas_call | solution.py:318
  60.0 1.8 %emit.1 = bf16[256,8,128]{2,1,0:T(8,128)(2,1)} custom-call(f32[8,128,128]{2,1,0:T(8,128)S(1)} %get-tuple-element.9.in_ref, f32[8,256,128]{2,1,0:T(8,128)S(1)} %get-tuple-element.10.lo_ref, bf16[8,256,128]{2,1,0:T(8,128)(2,1)S(1)} %get-tuple-element.11.qh_ref, bf16[8,256,128]{2,1,0:T(8,128)(2,1)S(1)} %get-tuple-element.12.ql_ref), custom_call_target="tpu_custom_call" | custom-call | tf_op jit(solution)/shard_map/emit/pallas_call | solution.py:343
Async XLA Ops:
  0.8 1.0 %copy-start = (bf16[256,8,128]{2,1,0:T(8,128)(2,1)S(1)}, bf16[256,8,128]{2,1,0:T(8,128)(2,1)}, u32[]{:S(2)}) copy-start(bf16[256,8,128]{2,1,0:T(8,128)(2,1)} %q_ref.1) | copy-start | bytes 1572868
  1.9 1.0 %copy-start.1 = (bf16[256,8,128]{2,1,0:T(8,128)(2,1)S(1)}, bf16[256,8,128]{2,1,0:T(8,128)(2,1)}, u32[]{:S(2)}) copy-start(bf16[256,8,128]{2,1,0:T(8,128)(2,1)} %k_ref.1) | copy-start | bytes 1572868
  2.9 1.0 %copy-start.2 = (bf16[256,8,128]{2,1,0:T(8,128)(2,1)S(1)}, bf16[256,8,128]{2,1,0:T(8,128)(2,1)}, u32[]{:S(2)}) copy-start(bf16[256,8,128]{2,1,0:T(8,128)(2,1)} %v_ref.1) | copy-start | bytes 1572868

commit v6 on v5

--- a/solution.py
+++ b/solution.py
@@ -125,9 +125,9 @@
 
 
 def maps_kernel(
-    segs, inners, q_ref, k_ref, v_ref, s_ref, in_ref, lo_ref, qh_ref, ql_ref,
+    segs, inners, q_ref, k_ref, v_ref, s_ref, out_ref, in_ref, lo_ref, qh_ref, ql_ref,
     wide, qs, ks, vs, solved, scale, own, earlier, pair_h, pair_l, pair_o, landed, leaving,
-    map_send, map_recv, next_send, fan_send, state_recv,
+    staged, map_send, map_recv, next_send, fan_send, state_recv, load_sem,
 ):
     heads = q_ref.shape[1]
     wide_k = own.shape[2]
@@ -165,8 +165,15 @@
     def fan_hop(h):
         return send(landed, landed, fan_send, state_recv, h, -1)
 
-    for source, target in ((k_ref, ks), (v_ref, vs), (q_ref, qs)):
-        wide[...] = source[...].astype(F32)
+    loads = [
+        pltpu.make_async_copy(source, staged.at[i], load_sem.at[i])
+        for i, source in enumerate((k_ref, v_ref, q_ref))
+    ]
+    for load in loads:
+        load.start()
+    for i, target in enumerate((ks, vs, qs)):
+        loads[i].wait()
+        wide[...] = staged[i].astype(F32)
         for h in range(heads):
             target[h] = wide[:, h, :].astype(BF16)
     strengths = s_ref[...]
@@ -297,6 +304,8 @@
                 fan_hop(h).wait_recv()
             in_ref[...] = landed[...]
 
+    emit_kernel(in_ref, lo_ref, qh_ref, ql_ref, out_ref, wide)
+
 
 def emit_kernel(in_ref, lo_ref, qh_ref, ql_ref, out_ref, wide):
     heads = in_ref.shape[0]
@@ -310,22 +319,20 @@
     wide_v = values.shape[2]
     vm = pl.BlockSpec(memory_space=pltpu.VMEM)
     shape = jax.ShapeDtypeStruct
-    params = pltpu.CompilerParams(vmem_limit_bytes=VMEM_LIMIT)
     dma = pltpu.SemaphoreType.DMA((heads,))
     maps = pltpu.VMEM((heads, width + wide_v, width), F32)
     halves = pltpu.VMEM((heads, width, width), BF16)
     states = pltpu.VMEM((heads, wide_v, width), F32)
-    entering, local, qh, ql = pl.pallas_call(
+    return pl.pallas_call(
         functools.partial(maps_kernel, segs, inners),
-        out_shape=[
-            shape((heads, wide_v, width), F32),
-            shape((heads, rows, wide_v), F32),
-            shape((heads, rows, width), BF16),
-            shape((heads, rows, width), BF16),
-        ],
-        in_specs=[vm] * 4,
-        out_specs=[vm] * 4,
+        out_shape=shape((rows, heads, wide_v), BF16),
+        in_specs=[pl.BlockSpec(memory_space=pltpu.HBM)] * 3 + [vm],
+        out_specs=vm,
         scratch_shapes=[
+            states,
+            pltpu.VMEM((heads, rows, wide_v), F32),
+            pltpu.VMEM((heads, rows, width), BF16),
+            pltpu.VMEM((heads, rows, width), BF16),
             pltpu.VMEM((rows, heads, width), F32),
             pltpu.VMEM((heads, rows, width), BF16),
             pltpu.VMEM((heads, rows, width), BF16),
@@ -333,22 +340,15 @@
             pltpu.VMEM((heads, rows, wide_v + width), F32),
             pltpu.VMEM((heads, 8, rows), F32),
             maps, maps, halves, halves, states, states, states,
+            pltpu.VMEM((3, rows, heads, width), BF16),
             dma, dma, dma, dma, dma,
+            pltpu.SemaphoreType.DMA((3,)),
         ],
         compiler_params=pltpu.CompilerParams(
-            collective_id=0, has_side_effects=True, vmem_limit_bytes=VMEM_LIMIT
+            collective_id=0, has_side_effects=True, vmem_limit_bytes=60 * 1024 * 1024
         ),
         name="maps_and_chain",
     )(queries, keys, values, strengths)
-    return pl.pallas_call(
-        emit_kernel,
-        out_shape=shape((rows, heads, wide_v), BF16),
-        in_specs=[vm] * 4,
-        out_specs=vm,
-        scratch_shapes=[pltpu.VMEM((rows, heads, wide_v), F32)],
-        compiler_params=params,
-        name="emit",
-    )(entering, local, qh, ql)
 
 
 def solution(mesh):

time: 62.2 us -> 62.8 us (level)
  Pallas kernels: 57.9 us -> 58.8 us
    pallas_call x2 -> x1, Pallas kernels: 57.9 us -> 58.8 us  [body(): pl.pallas_call(functools.partial(maps_kernel, segs, inners), out_shape=sh...]
    unnamed x7 -> x2, local copies, waits for them, and re-layouts: 3.94 us -> 3.35 us
where the time goes in v6:
time: 62.8 us; the launch traced here: 62.1 us
  Pallas kernels  58.8 us (94%)
  local copies, waits for them, and re-layouts  3.35 us (5%)
    pallas_call x1, Pallas kernels, body(): pl.pallas_call(functools.partial(maps_kernel, segs, inners), out_shape=sh...  58.8 us
    unnamed x2, local copies, waits for them, and re-layouts  3.35 us

profile of v6, /device:TPU:25, one launch (start us, length us, event | category | flops | bytes accessed | tf_op | source)
XLA Modules:
  0.0 62.1 jit_solution(4073989433740811624)
XLA Ops:
  0.0 1.5 %copy.5.s_ref = f32[256,8]{1,0:T(8,128)} copy(f32[256,8]{0,1:T(8,128)} %param.7) | data formatting | bytes 16384 | tf_op args[3]
  1.5 58.8 %maps_and_chain.1 = bf16[256,8,128]{2,1,0:T(8,128)(2,1)} custom-call(bf16[256,8,128]{2,1,0:T(8,128)(2,1)} %q_ref.1, bf16[256,8,128]{2,1,0:T(8,128)(2,1)} %k_ref.1, bf16[256,8,128]{2,1,0:T(8,128)(2,1)} %v_ref.1, f32[256,8]{1,0:T(8,128)} %copy.5.s_ref), custom_call_target="tpu_custom_call" | custom-call | tf_op jit(solution)/shard_map/maps_and_chain/pallas_call | solution.py:326
  60.3 1.9 %copy.7 = bf16[256,8,128]{2,1,0:T(8,128)(2,1)} copy(bf16[256,8,128]{2,1,0:T(8,128)(2,1)} %maps_and_chain.1) | data formatting | bytes 1048576
